TPU v7x, 32 devices: a whole 2x2x4 slice. The times are simulated.
32 devices in a mesh: section: 2 (over x), dp: 16 (over z, y, core).
Axes of the slice: x: 2, y: 2, z: 4, core: 2. Of those that a mesh axis runs over, the one named last changes fastest.
Arguments:
- block_in: bfloat16 [2, 32, 256, 768], P('section', 'dp'), may hold values from -6 to 6
- cotangent: bfloat16 [32, 256, 768], P('dp'), may hold values from -6 to 6
- lengths: int32 [32], P('dp'), may hold values from 63 to 256, as said below
- sources: int32 [32], P('dp'), may hold values from 0 to 2
- loss_weight: int32 [3], replicated, may hold values from 1 to 3
- gains: bfloat16 [2, 3, 768], P('section', None, 'dp'), may hold values from 0.5 to 1.5
- qkv_weight: bfloat16 [2, 768, 2304], P('section', 'dp'), may hold values from -0.21875 to 0.21875
- out_weight: bfloat16 [2, 768, 768], P('section', 'dp'), may hold values from -2.5 to 2.5
- cross_weight: bfloat16 [2, 768, 1536], P('section', 'dp'), may hold values from -2.5 to 2.5
- in_weight: bfloat16 [2, 768, 4096], P('section', 'dp'), may hold values from -0.21875 to 0.21875
- down_weight: bfloat16 [2, 2048, 768], P('section', 'dp'), may hold values from -0.125 to 0.125
Outputs:
- block_out: bfloat16 [2, 32, 256, 768], P('section', 'dp')
- input_grad: float32 [2, 32, 256, 768], P('section', 'dp')
- gains_grad: float32 [2, 3, 768], P('section', None, 'dp')
- qkv_grad: float32 [2, 768, 2304], P('section', 'dp')
- out_grad: float32 [2, 768, 768], P('section', 'dp')
- cross_grad: float32 [2, 768, 1536], P('section', 'dp')
- in_grad: float32 [2, 768, 4096], P('section', 'dp')
- down_grad: float32 [2, 2048, 768], P('section', 'dp')
Inputs may be any that keep to these rules, and one draw needn't show every extreme that they name: `lengths`: in every draw some table has exactly 256 tokens.
All inputs are finite; a program needn't handle non-finite values.
Results may differ from a plain program's by a relative error of at most 0.015.
Values may be sent and summed in bfloat16 or wider, within the bound.
A program may use at most 384 MiB of HBM per device.

v0:
```python
from functools import partial

import jax
import jax.numpy as jnp
from jax import lax
from jax.experimental import pallas as pl
from jax.experimental.pallas import tpu as pltpu
from jax.sharding import PartitionSpec as P

HEADS = 12
HEAD_DIM = 64


EPS = 1e-06
NEG = -1000000000.0


MESH = pl.DeviceIdType.MESH
VMEM_LIMIT = 62 * 2**20
F32, BF16 = jnp.float32, jnp.bfloat16
ANY = pl.BlockSpec(memory_space=pl.ANY)
SMEM = pl.BlockSpec(memory_space=pltpu.SMEM)
VMEM = pl.BlockSpec(memory_space=pltpu.VMEM)


def ring_position(chip, chips):
    return jnp.where(chip % 2 == 0, chip // 2, chips - 1 - chip // 2)


def ring_chip(position, chips):
    position = lax.rem(position + 2 * chips, chips)
    return jnp.where(position < chips // 2, 2 * position, 2 * (chips - 1 - position) + 1)


def ring_hops(long_way, chips):
    long, short = chips // 2, chips - 1 - chips // 2
    return (long, short) if long_way == 0 else (short, long)


def slot_of(long_way, way, distance, chips):
    return distance if distance == 0 or way == long_way else chips // 2 + distance


def entry_barrier(partners):
    barrier = pltpu.get_barrier_semaphore()
    for partner in partners:
        pl.semaphore_signal(barrier, inc=1, device_id=partner, device_id_type=MESH)
    pl.semaphore_wait(barrier, len(partners))


def remote(src, dst, send_sem, recv_sem, target):
    return pltpu.make_async_remote_copy(
        src_ref=src,
        dst_ref=dst,
        send_sem=send_sem,
        recv_sem=recv_sem,
        device_id=target,
        device_id_type=MESH,
    )


class Place:
    def __init__(self, wide):
        self.chips = wide // 2
        self.section, self.me = lax.axis_index("section"), lax.axis_index("dp")
        self.chip, self.core = self.me // 2, lax.rem(self.me, 2)
        self.spot = ring_position(self.chip, self.chips)
        self.ahead = (self.section, 2 * ring_chip(self.spot + 1, self.chips) + self.core)
        self.behind = (self.section, 2 * ring_chip(self.spot - 1, self.chips) + self.core)
        self.twin = (self.section, 2 * self.chip + 1 - self.core)
        self.across = (1 - self.section, self.me)

    def next_of(self, way):
        return self.ahead if way == 0 else self.behind

    def chip_at(self, way, distance):
        return ring_chip(self.spot + distance if way == 0 else self.spot - distance, self.chips)


def block_rows(ref, rows, chip, core):
    return ref.at[pl.ds(pl.multiple_of((2 * chip + core) * rows, rows), rows)]


class Gather:
    def __init__(self, place, names, shards, fulls, rows, long_way, sems):
        self.place, self.names = place, names
        self.shards, self.fulls, self.rows, self.long_way = shards, fulls, rows, long_way
        self.own_sem, self.ring_send, self.ring_recv, self.twin_send, self.twin_recv = sems

    def hops(self, name, way):
        return ring_hops(self.long_way[name], self.place.chips)[way]

    def pieces(self, name, way, hop):
        at = self.place
        origin = at.chip_at(way, -hop)
        target = block_rows(self.fulls[name], self.rows[name], origin, at.core)
        own = self.shards.get(name)
        return (own if hop == 0 and own is not None else target), target

    def ring(self, name, way, hop):
        source, target = self.pieces(name, way, hop)
        i = self.names.index(name)
        return remote(
            source, target, self.ring_send.at[i, way, hop], self.ring_recv.at[i, way, hop], self.place.next_of(way)
        )

    def pair(self, name, way, hop):
        source, target = self.pieces(name, way, hop)
        i, slot = self.names.index(name), slot_of(self.long_way[name], way, hop, self.place.chips)
        return remote(source, target, self.twin_send.at[i, slot], self.twin_recv.at[i, slot], self.place.twin)

    def own(self, name):
        source, target = self.pieces(name, 0, 0)
        return pltpu.make_async_copy(source, target, self.own_sem.at[self.names.index(name)])

    def start(self, name):
        for way in range(2):
            self.ring(name, way, 0).start()
        self.pair(name, 0, 0).start()
        if name in self.shards:
            self.own(name).start()

    def step(self, name, hop):
        for way in range(2):
            hops = self.hops(name, way)
            if hop < hops:
                self.ring(name, way, hop).wait_recv()
                if hop + 1 < hops:
                    self.ring(name, way, hop + 1).start()
                self.pair(name, way, hop + 1).start()

    def complete(self, name):
        if name in self.shards:
            self.own(name).wait()
        self.pair(name, 0, 0).wait_recv()
        for way in range(2):
            for hop in range(self.hops(name, way)):
                self.pair(name, way, hop + 1).wait_recv()

    def drain(self, names):
        for name in names:
            self.pair(name, 0, 0).wait_send()
            for way in range(2):
                for hop in range(self.hops(name, way)):
                    self.pair(name, way, hop + 1).wait_send()
                    self.ring(name, way, hop).wait_send()


LONG_WAY = {"small": 0, "qkv": 0, "out": 1, "crossE": 0, "crossD": 1, "in": 1, "down": 0, "gains": 0}


class Scatter:
    def __init__(self, place, names, grads, rows, long_way, twins, arrived, sems):
        self.place, self.names, self.grads, self.rows, self.long_way = place, names, grads, rows, long_way
        self.twins, self.arrived = twins, arrived
        self.twin_send, self.twin_recv, self.ring_send, self.ring_recv = sems

    def hops(self, name, way):
        return ring_hops(self.long_way[name], self.place.chips)[way]

    def landing(self, name, way, hop):
        return self.arrived[name].at[hop if way == self.long_way[name] else self.place.chips // 2 + hop]

    def block(self, name, way, distance, core):
        return block_rows(self.grads[name], self.rows[name], self.place.chip_at(way, distance), core)

    def pair(self, name, way, distance):
        at, i = self.place, self.names.index(name)
        slot = slot_of(self.long_way[name], way, distance, at.chips)
        source = self.block(name, way, distance, 1 - at.core)
        return remote(source, self.twins[name].at[slot], self.twin_send.at[i, slot], self.twin_recv.at[i, slot], at.twin)

    def ring(self, name, way, hop):
        at, i = self.place, self.names.index(name)
        return remote(
            self.block(name, way, self.hops(name, way) - hop, at.core),
            self.landing(name, way, hop),
            self.ring_send.at[i, way, hop],
            self.ring_recv.at[i, way, hop],
            at.next_of(way),
        )

    def slots(self, name):
        found = []
        for hop in range(self.place.chips // 2 + 1):
            for way in range(2):
                distance = self.hops(name, way) - hop
                if distance > 0 or (distance == 0 and way == self.long_way[name]):
                    found.append((way, distance))
        return found

    def start(self, name):
        for way, distance in self.slots(name):
            self.pair(name, way, distance).start()

    def add(self, name, way, distance, terms, out=None):
        at, rows, grad = self.place, self.rows[name], self.grads[name]
        group = 16 if rows % 16 == 0 else rows
        tile = next(t for t in (1024, 768, 128) if grad.shape[1] % t == 0)
        first = (2 * at.chip_at(way, distance) + at.core) * rows
        slot = slot_of(self.long_way[name], way, distance, at.chips)

        @pl.loop(0, rows // group)
        def _(n):
            part = span(n * group, group)
            own = pl.ds(pl.multiple_of(first + n * group, group), group)

            @pl.loop(0, grad.shape[1] // tile)
            def _(m):
                columns = span(m * tile, tile)
                total = grad[own, columns].astype(F32) + self.twins[name][slot, part, columns].astype(F32)
                for term in terms:
                    total += term[part, columns].astype(F32)
                if out is None:
                    grad[own, columns] = total.astype(grad.dtype)
                else:
                    out[part, columns] = total

    def step(self, name, way, hop):
        distance = self.hops(name, way) - hop
        if distance <= 0:
            return
        self.pair(name, way, distance).wait_recv()
        terms = []
        if hop > 0:
            self.ring(name, way, hop - 1).wait_recv()
            terms.append(self.landing(name, way, hop - 1))
        self.add(name, way, distance, terms)
        self.ring(name, way, hop).start()

    def finish(self, name, out):
        self.pair(name, self.long_way[name], 0).wait_recv()
        terms = []
        for way in range(2):
            last = self.hops(name, way) - 1
            self.ring(name, way, last).wait_recv()
            terms.append(self.landing(name, way, last))
        self.add(name, self.long_way[name], 0, terms, out)

    def drain(self, name):
        for way, distance in self.slots(name):
            self.pair(name, way, distance).wait_send()
        for way in range(2):
            for hop in range(self.hops(name, way)):
                self.ring(name, way, hop).wait_send()


def dot(a, b, over_a=1, over_b=0):
    return lax.dot_general(a, b, (((over_a,), (over_b,)), ((), ())), preferred_element_type=F32)


def span(start, size):
    return pl.ds(start, size) if isinstance(start, int) else pl.ds(pl.multiple_of(start, size), size)


def each(total, tile, work):
    @pl.loop(0, total // tile)
    def _(n):
        work(span(n * tile, tile))


ROWS = 64


def norm_into(h_ref, gain, out_ref):
    def work(at):
        h = h_ref[at].astype(F32)
        inv_root = lax.rsqrt(jnp.mean(h * h, axis=-1, keepdims=True) + EPS)
        out_ref[at] = (h * inv_root * gain).astype(out_ref.dtype)

    each(h_ref.shape[0], ROWS, work)


def norm_back(dn_ref, h_ref, gain, gain_sum, row, finish, start=0, size=None):
    if start == 0:
        gain_sum[row] = jnp.zeros(gain_sum.shape[1:], F32)

    def work(part):
        at = span(start + part.start, ROWS)
        h, dn = h_ref[at].astype(F32), dn_ref[at].astype(F32)
        inv_root = lax.rsqrt(jnp.mean(h * h, axis=-1, keepdims=True) + EPS)
        scaled = h * inv_root
        product = dn * scaled
        gain_sum[row] += jnp.sum(product.reshape(-1, 8, product.shape[1]), axis=0)
        inner = dn * gain
        finish(at, inv_root * (inner - scaled * jnp.mean(product * gain, axis=-1, keepdims=True)))

    each(size or h_ref.shape[0], ROWS, work)


def pair_columns(ref, rows, start, two):
    return ref[rows, span(start + two * 2 * HEAD_DIM, 2 * HEAD_DIM)]


def side_masks():
    lane = lax.broadcasted_iota(jnp.int32, (1, 2 * HEAD_DIM), 1)
    first = lane < HEAD_DIM
    return first, (first.astype(F32).astype(BF16), (1 - first.astype(F32)).astype(BF16))


def expo_columns(q, k, seq, length):
    scores = dot(k, q, 1, 1) * HEAD_DIM ** (-0.5)
    if length is not None:
        key = lax.broadcasted_iota(jnp.int32, (seq, seq), 0)
        query = lax.broadcasted_iota(jnp.int32, (seq, seq), 1)
        scores = jnp.where((key <= query) & (key < length), scores, NEG)
    expo = jnp.exp(scores - jnp.max(scores, axis=0, keepdims=True))
    return expo, jnp.sum(expo, axis=0, keepdims=True)


def attend(q_ref, q_at, k_ref, k_at, v_ref, v_at, out_ref, seq, lengths, chosen=None):
    start, stop = chosen or (0, q_ref.shape[0] // seq)
    first, keeps = side_masks()
    each_time = HEADS // 4

    @pl.loop(start * (HEADS // 2 // each_time), stop * (HEADS // 2 // each_time))
    def _(m):
        work = []
        for g in range(each_time):
            n = m * each_time + g
            pair, two = n // (HEADS // 2), lax.rem(n, HEADS // 2)
            rows = span(pair * seq, seq)
            length = None if lengths is None else lengths[pair]
            q, k, v = (pair_columns(r, rows, a, two) for r, a in ((q_ref, q_at), (k_ref, k_at), (v_ref, v_at)))
            for side in range(2):
                work.append((rows, two, length, q, k, v, side))
        expos = [expo_columns(q * keeps[side], k, seq, length) for rows, two, length, q, k, v, side in work]
        outs = [dot((e * (1.0 / t)).astype(BF16), w[5], 0, 0) for (e, t), w in zip(expos, work)]
        for g in range(each_time):
            rows, two = work[2 * g][:2]
            value = jnp.where(first, outs[2 * g], outs[2 * g + 1])
            out_ref[rows, span(two * 2 * HEAD_DIM, 2 * HEAD_DIM)] = value.astype(BF16)


def attend_back(q_ref, q_at, k_ref, k_at, v_ref, v_at, do_ref, dq, dk, dv, seq, lengths, chosen=None):
    start, stop = chosen or (0, q_ref.shape[0] // seq)
    first, keeps = side_masks()
    root = HEAD_DIM ** (-0.5)
    each_time = HEADS // 6

    @pl.loop(start * (HEADS // 2 // each_time), stop * (HEADS // 2 // each_time))
    def _(m):
        work = []
        for g in range(each_time):
            n = m * each_time + g
            pair, two = n // (HEADS // 2), lax.rem(n, HEADS // 2)
            rows = span(pair * seq, seq)
            length = None if lengths is None else lengths[pair]
            q, k, v = (pair_columns(r, rows, a, two) for r, a in ((q_ref, q_at), (k_ref, k_at), (v_ref, v_at)))
            d_out = pair_columns(do_ref, rows, 0, two)
            for side in range(2):
                work.append((rows, two, length, q, k, v, d_out, side))
        expos = [expo_columns(q * keeps[side], k, seq, length) for rows, two, length, q, k, v, d_out, side in work]
        d_probs = [dot(v, d_out * keeps[side], 1, 1) for rows, two, length, q, k, v, d_out, side in work]
        probs = [e * (1.0 / t) for e, t in expos]
        d_scores = [(p * (d - jnp.sum(p * d, axis=0, keepdims=True))).astype(BF16) for p, d in zip(probs, d_probs)]
        dvs = [dot(p.astype(BF16), w[6]) for p, w in zip(probs, work)]
        dqs = [dot(d, w[4], 0, 0) for d, w in zip(d_scores, work)]
        dks = [dot(d, w[3]) for d, w in zip(d_scores, work)]
        for g in range(each_time):
            rows, two = work[2 * g][:2]
            for (ref, start), both, factor in ((dq, dqs, root), (dk, dks, root), (dv, dvs, 1.0)):
                value = jnp.where(first, both[2 * g], both[2 * g + 1]) * factor
                ref[rows, span(start + two * 2 * HEAD_DIM, 2 * HEAD_DIM)] = value.astype(BF16)


def gelu_parts(gate):
    root, cubic = 0.7978845608028654, 0.044715
    square = gate * gate
    bent = jnp.tanh(root * gate * (1.0 + cubic * square))
    half = 0.5 * (1.0 + bent)
    slope = half + 0.5 * gate * (1.0 - bent * bent) * root * (1.0 + 3.0 * cubic * square)
    return gate * half, slope


FF_TILE = 512


def mlp_forward(a_ref, w_in, w_down, into_ref, hidden_ref=None, slopes_ref=None):
    ff = w_in.shape[1] // 2

    @pl.loop(0, ff // FF_TILE)
    def _(n):
        gates, uppers = span(n * FF_TILE, FF_TILE), span(ff + n * FF_TILE, FF_TILE)
        gate, upper = dot(a_ref[...], w_in[:, gates]), dot(a_ref[...], w_in[:, uppers])
        active, slope = gelu_parts(gate)
        hidden = (active * upper).astype(BF16)
        if hidden_ref is not None:
            hidden_ref[:, gates] = hidden
            slopes_ref[:, gates] = (slope * upper).astype(BF16)
            slopes_ref[:, uppers] = active.astype(BF16)
        if w_down is not None:
            into_ref[...] += dot(hidden, w_down[gates, :])


def mlp_back(d_low, w_in, w_down, slopes_ref, dn_ref):
    ff = w_in.shape[1] // 2
    dn_ref[...] = jnp.zeros(dn_ref.shape, F32)

    @pl.loop(0, ff // FF_TILE)
    def _(n):
        gates, uppers = span(n * FF_TILE, FF_TILE), span(ff + n * FF_TILE, FF_TILE)
        d_hidden = dot(d_low[...], w_down[gates, :], 1, 1)
        d_gate = (d_hidden * slopes_ref[:, gates]).astype(BF16)
        d_upper = (d_hidden * slopes_ref[:, uppers]).astype(BF16)
        slopes_ref[:, gates], slopes_ref[:, uppers] = d_gate, d_upper
        dn_ref[...] += dot(d_gate, w_in[:, gates], 1, 1) + dot(d_upper, w_in[:, uppers], 1, 1)


def product_into(a_ref, w_ref, out_ref, tile, w_at=0, transposed=False):
    width = out_ref.shape[1]

    @pl.loop(0, width // tile)
    def _(n):
        if transposed:
            value = dot(a_ref[...], w_ref[span(w_at + n * tile, tile), :], 1, 1)
        else:
            value = dot(a_ref[...], w_ref[:, span(w_at + n * tile, tile)])
        out_ref[:, span(n * tile, tile)] = value.astype(out_ref.dtype)


def add_product(base_ref, a_ref, w, out_ref):
    out_ref[...] = base_ref[...].astype(F32) + dot(a_ref[...], w)


class Moves:
    def __init__(self, sems):
        self.sems, self.used = sems, 0

    def start(self, src, dst):
        copy = pltpu.make_async_copy(src, dst, self.sems.at[self.used])
        self.used += 1
        copy.start()
        return copy


def weight_grad(a_ref, y_ref, grad, tile_rows, tile_columns, column_at=0):
    @pl.loop(0, a_ref.shape[1] // tile_rows)
    def _(i):
        @pl.loop(0, y_ref.shape[1] // tile_columns)
        def _(j):
            rows, columns = span(i * tile_rows, tile_rows), span(j * tile_columns, tile_columns)
            value = dot(a_ref[:, rows], y_ref[:, columns], 0, 0).astype(BF16)
            grad[rows, pl.ds(pl.multiple_of(column_at + j * tile_columns, 256), tile_columns)] = value


GATHER_NAMES = ("small", "qkv", "out", "crossE", "crossD", "in", "down")
SCATTER_NAMES = ("down", "in", "crossD", "crossE", "out", "qkv", "gains")
BLOCK = (8, 128)


def spread_gains(small, own, width):
    lane = lax.broadcasted_iota(jnp.int32, BLOCK, 1)
    total = jnp.zeros((BLOCK[0], width), F32)
    for n in range(width // own):
        part = jnp.where(lane < own, small[n * BLOCK[0] : (n + 1) * BLOCK[0], :], 0.0)
        wide = jnp.concatenate([part, jnp.zeros((BLOCK[0], width - BLOCK[1]), F32)], axis=1)
        total += wide if n == 0 else pltpu.roll(wide, n * own, 1)
    return total


def gather_blocks(gains_grad, own, out_ref):
    width = gains_grad.shape[1]
    lane = lax.broadcasted_iota(jnp.int32, BLOCK, 1)
    for n in range(width // own):
        turned = gains_grad if n == 0 else pltpu.roll(gains_grad, width - n * own, 1)
        out_ref[n * BLOCK[0] : (n + 1) * BLOCK[0], :] = jnp.where(lane < own, turned[:, : BLOCK[1]], 0.0)


def step_kernel(
    wide, seq, lengths, sources, loss_weight, gains_in, x_in, cot_in, qkv_in, out_in, cross_in, in_in, down_in,
    small_full, qkv_full, out_full, enc_full, dec_full, in_full, down_full,
    joined_kept, attended_kept, middle_kept, final_kept,
    block_out, input_out, down_sum, in_sum, cross_sum, out_sum, qkv_sum, gains_sum,
    small_own, gains, factors, gain_sum, landing, back, passed_out, passed_in, g_gains, g_down, *refs,
):
    count = len(SCATTER_NAMES)
    twins, arrived = dict(zip(SCATTER_NAMES, refs[:count])), dict(zip(SCATTER_NAMES, refs[count : 2 * count]))
    load_sem, send_sem, recv_sem = refs[2 * count : 2 * count + 3]
    gather_sems, scatter_sems = refs[2 * count + 3 : 2 * count + 8], refs[2 * count + 8 :]
    at = Place(wide)
    rows, width = x_in.shape
    pairs, own = rows // seq, gains_in.shape[1]
    vmem = pltpu.VMEM
    broad, slim = vmem((rows, width), F32), vmem((rows, width), BF16)
    lane = lax.broadcasted_iota(jnp.int32, (1, BLOCK[1]), 1)
    counted = jnp.zeros((1, BLOCK[1]), F32)
    for pair in range(pairs):
        counted += jnp.where(lane == sources[pair], lengths[pair].astype(F32), 0.0)
    small_own[...] = jnp.zeros(BLOCK, F32)
    small_own[0:3, 0:own] = gains_in[...].astype(F32)
    small_own[3:4, :] = counted
    entry_barrier((at.ahead, at.behind, at.twin, at.across))

    fulls = dict(zip(GATHER_NAMES, (small_full, qkv_full, out_full, enc_full, dec_full, in_full, down_full)))
    full_rows = {n: f.shape[0] // wide for n, f in fulls.items()}
    w_qkv_shape, w_out_shape, w_cross_shape = qkv_full.shape, out_full.shape, dec_full.shape
    w_in_shape, w_down_shape = in_full.shape, down_full.shape
    ff = w_down_shape[0]
    shapes = dict(zip(SCATTER_NAMES, (w_down_shape, w_in_shape, w_cross_shape, w_cross_shape, w_out_shape, w_qkv_shape)))
    shapes["gains"] = g_gains.shape
    share = {n: s[0] // wide for n, s in shapes.items()}
    grads = {"down": g_down, "gains": g_gains}
    scatter = Scatter(at, SCATTER_NAMES, grads, share, LONG_WAY, twins, arrived, scatter_sems)
    sums = {"down": down_sum, "in": in_sum, "out": out_sum, "qkv": qkv_sum, "gains": gains_sum}
    sums.update(crossD=cross_sum, crossE=passed_out)
    passed_weight = remote(
        cross_in, block_rows(enc_full, full_rows["crossE"], at.chip, at.core), send_sem.at[0], recv_sem.at[0], at.across
    )
    passed_sum = remote(passed_out, passed_in, send_sem.at[1], recv_sem.at[1], at.across)

    def grad_space(*names):
        return [vmem(shapes[n], BF16) for n in names]

    def to_dec(pair):
        part = span(pair * seq, seq)
        return remote(back.at[part], landing.at[part], send_sem.at[2 + pair], recv_sem.at[2 + pair], at.across)

    def to_enc(pair):
        part, i = span(pair * seq, seq), 2 + pairs + pair
        return remote(back.at[part], landing.at[part], send_sem.at[i], recv_sem.at[i], at.across)

    class Hops:
        def __init__(self):
            self.done = {}

        def hop(self, *names):
            for name in names:
                for way in range(2):
                    scatter.step(name, way, self.done.get(name, 0))
                self.done[name] = self.done.get(name, 0) + 1

        def ready(self, name):
            scatter.start(name)
            self.hop(name)

        def rest(self, names):
            for step in range(at.chips // 2 + 1):
                for name in names:
                    if self.done[name] == step < at.chips // 2:
                        self.hop(name)
                    elif self.done[name] == step:
                        scatter.finish(name, sums[name])
                        self.done[name] += 1
                        if name == "crossE":
                            passed_sum.start()

    def first_part(moves, gather, names, lengths, x, small, w_qkv, w_out, normed, joined, attended, middle, between):
        load_x = moves.start(x_in, x)
        for name in names:
            if name == "crossE":
                passed_weight.wait_recv()
            gather.start(name)
        for hop in range(at.chips // 2 - 1):
            for name in names:
                gather.step(name, hop)

        def load(name, into):
            gather.complete(name)
            return moves.start(fulls[name], into)

        gather.step("small", at.chips // 2 - 1)
        load("small", small).wait()
        gains[...] = spread_gains(small, own, width)
        totals = jnp.zeros((1, BLOCK[1]), F32)
        for n in range(wide):
            totals += small[n * BLOCK[0] + 3 : n * BLOCK[0] + 4, :]
        factors[...] = jnp.zeros(factors.shape, F32)
        for pair in range(pairs):
            source = sources[pair]
            weight = jnp.where(source == 0, loss_weight[0], jnp.where(source == 1, loss_weight[1], loss_weight[2]))
            total = jnp.sum(jnp.where(lane == source, totals, 0.0), axis=1, keepdims=True)
            factor = jnp.full((1, 1), weight.astype(F32) * (pairs * wide * seq / 3.0), F32) / total
            factors[pair : pair + 1, :] = jnp.broadcast_to(factor, (1, BLOCK[1]))
        load_x.wait()
        norm_into(x, gains[0:1], normed)
        gather.step("qkv", at.chips // 2 - 1)
        gather.step("out", at.chips // 2 - 1)
        load_qkv = load("qkv", w_qkv)
        load_out = load("out", w_out)
        load_qkv.wait()
        product_into(normed, w_qkv, joined, width)
        for name in names[3:]:
            gather.step(name, at.chips // 2 - 1)
        between()
        attend(joined, 0, joined, width, joined, 2 * width, attended, seq, lengths)
        load_out.wait()
        add_product(x, attended, w_out[...], middle)
        return [moves.start(a, b) for a, b in ((middle, middle_kept), (joined, joined_kept), (attended, attended_kept))]

    def self_back(hops, lengths, d_middle, x, normed, d_low, w_qkv, w_out, joined, attended, d_attended, dn, loads, first, second):
        each(rows, ROWS, lambda part: d_low.__setitem__(part, d_middle[part].astype(BF16)))
        weight_grad(attended, d_low, grads["out"], width // 3, width)
        hops.ready("out")
        product_into(d_low, w_out, d_attended, width, transposed=True)
        hops.hop(*first)
        for load in loads:
            load.wait()
        attend_back(
            joined, 0, joined, width, joined, 2 * width, d_attended,
            (joined, 0), (joined, width), (joined, 2 * width), seq, lengths,
        )
        hops.hop(*second)
        norm_into(x, gains[0:1], normed)
        weight_grad(normed, joined, grads["qkv"], width // 3, width)
        hops.ready("qkv")
        product_into(joined, w_qkv, dn, width, transposed=True)

        def finish(part, d_input):
            d_middle[part] = d_middle[part] + d_input

        norm_back(dn, x, gains[0:1], gain_sum, 0, finish)

    def gains_ready(hops):
        lines = [jnp.sum(gain_sum[row], axis=0, keepdims=True) for row in range(3)]
        gather_blocks(jnp.concatenate(lines + [jnp.zeros((BLOCK[0] - 3, width), F32)], axis=0), own, g_gains)
        hops.ready("gains")

    @pl.when(at.section == 0)
    def _():
        moves, hops = Moves(load_sem), Hops()
        passed_weight.start()
        names = ("small", "qkv", "out", "in", "down")
        shards = dict(zip(names, (small_own, qkv_in, out_in, in_in, down_in)))
        gather = Gather(at, GATHER_NAMES, shards, fulls, full_rows, LONG_WAY, gather_sems)

        def ahead(x, small, w_qkv, w_out, normed, joined, attended, middle, w_in, w_down):
            loads = []

            def between():
                for name, into in (("in", w_in), ("down", w_down)):
                    gather.complete(name)
                    loads.append(moves.start(fulls[name], into))

            stores = first_part(
                moves, gather, names, None, x, small, w_qkv, w_out, normed, joined, attended, middle, between
            )
            norm_into(middle, gains[1:2], normed)
            for copy in loads + stores[:1]:
                copy.wait()
            mlp_forward(normed, w_in, w_down, middle)
            stores.append(moves.start(middle, final_kept))
            for pair in range(pairs):
                part = pl.ds(pair * seq, seq)
                norm_into(middle.at[part], gains[2:3], back.at[part])
                to_dec(pair).start()
            stores.append(moves.start(back, block_out))
            for copy in stores[1:]:
                copy.wait()

        pl.run_scoped(
            ahead,
            slim, vmem(small_full.shape, F32), vmem(w_qkv_shape, BF16), vmem(w_out_shape, BF16),
            slim, vmem((rows, 3 * width), BF16), slim, broad, vmem(w_in_shape, BF16), vmem(w_down_shape, BF16),
        )

        def backward(final, normed, w_out, attended, g_in, g_out, g_qkv):
            grads.update({"in": g_in, "out": g_out, "qkv": g_qkv})
            early = [moves.start(a, b) for a, b in ((out_full, w_out), (attended_kept, attended))]

            def feed(w_in, w_down, middle, hidden, slopes, d_low, dn):
                loads = [
                    moves.start(a, b)
                    for a, b in ((middle_kept, middle), (in_full, w_in), (final_kept, final), (down_full, w_down))
                ]
                for load in loads:
                    load.wait()
                norm_into(middle, gains[1:2], normed)
                mlp_forward(normed, w_in, None, None, hidden, slopes)

                def finish_final(part, d_input):
                    final[part] = d_input
                    d_low[part] = d_input.astype(BF16)

                for pair in range(pairs):
                    to_enc(pair).wait_recv()
                    norm_back(landing, final, gains[2:3], gain_sum, 2, finish_final, pair * seq, seq)
                weight_grad(hidden, d_low, g_down, ff // 4, width)
                hops.ready("down")
                mlp_back(d_low, w_in, w_down, slopes, dn)
                hops.hop("down")
                weight_grad(normed, slopes, g_in, width // 3, ff // 2)
                hops.ready("in")
                hops.hop("down")

                def finish_middle(part, d_input):
                    final[part] = final[part] + d_input

                norm_back(dn, middle, gains[1:2], gain_sum, 1, finish_middle)

            pl.run_scoped(
                feed,
                vmem(w_in_shape, BF16), vmem(w_down_shape, BF16), broad, vmem((rows, ff), BF16), vmem((rows, 2 * ff), BF16),
                slim, broad,
            )

            def attention(w_qkv, x, joined, d_low, d_attended, dn):
                loads = [moves.start(a, b) for a, b in ((joined_kept, joined), (x_in, x), (qkv_full, w_qkv))]
                for load in early:
                    load.wait()
                self_back(
                    hops, None, final, x, normed, d_low, w_qkv, w_out, joined, attended, d_attended, dn, loads, ("in",), ("out", "in")
                )
                store = moves.start(final, input_out)
                gains_ready(hops)
                hops.rest(("down", "in", "out", "qkv", "gains"))
                store.wait()

            pl.run_scoped(
                attention,
                vmem(w_qkv_shape, BF16), slim, vmem((rows, 3 * width), BF16), slim, slim, broad,
            )
            for name in ("down", "in", "out", "qkv", "gains"):
                scatter.drain(name)

        pl.run_scoped(backward, broad, slim, vmem(w_out_shape, BF16), slim, *grad_space("in", "out", "qkv"))
        gather.drain(names)
        passed_weight.wait_send()
        for pair in range(pairs):
            to_dec(pair).wait_send()
        passed_sum.wait_recv()
        cross_sum[...] = passed_in[...]

    @pl.when(at.section == 1)
    def _():
        moves, hops = Moves(load_sem), Hops()
        names = ("small", "qkv", "out", "crossD", "crossE", "in", "down")
        shards = {"small": small_own, "qkv": qkv_in, "out": out_in, "crossD": cross_in, "in": in_in, "down": down_in}
        gather = Gather(at, GATHER_NAMES, shards, fulls, full_rows, LONG_WAY, gather_sems)

        def ahead(x, small, w_qkv, w_out, normed, joined, attended, middle):
            stores = first_part(
                moves, gather, names, lengths, x, small, w_qkv, w_out, normed, joined, attended, middle, lambda: None
            )
            for store in stores:
                store.wait()

        pl.run_scoped(
            ahead,
            slim, vmem(small_full.shape, F32), vmem(w_qkv_shape, BF16), vmem(w_out_shape, BF16),
            slim, vmem((rows, 3 * width), BF16), slim, broad,
        )

        def rest(cot, normed_a, keyval, crossed, normed_b, slopes, d_low2, d_after):
            d_queries, d_keyval, memory = cot, keyval, landing

            def to_memory(w_enc, w_dec, w_in, w_down, queries, after, hidden, d_low, dn, d_crossed, middle):
                load_middle = moves.start(middle_kept, middle)
                load_cot = moves.start(cot_in, cot)
                loads = []
                for name, into in (("crossD", w_dec), ("crossE", w_enc)):
                    gather.complete(name)
                    loads.append(moves.start(fulls[name], into))
                load_middle.wait()
                norm_into(middle, gains[1:2], normed_a)
                loads[0].wait()
                product_into(normed_a, w_dec, queries, width)
                loads[1].wait()
                for name, into in (("in", w_in), ("down", w_down)):
                    gather.complete(name)
                    loads.append(moves.start(fulls[name], into))

                @pl.loop(0, pairs)
                def _(pair):
                    part = span(pair * seq, seq)
                    to_dec(pair).wait_recv()
                    product_into(memory.at[part], w_enc, keyval.at[part], width)
                    attend(queries, 0, keyval, 0, keyval, width, crossed, seq, None, (pair, pair + 1))

                add_product(middle, crossed, w_dec[:, width:], after)
                norm_into(after, gains[2:3], normed_b)
                for load in loads[2:] + [load_cot]:
                    load.wait()
                dn[...] = after[...]
                mlp_forward(normed_b, w_in, w_down, dn, hidden, slopes)

                for pair in range(pairs):

                    @pl.loop(0, seq // ROWS)
                    def _(n):
                        part = span(pair * seq + n * ROWS, ROWS)
                        position = n * ROWS + lax.broadcasted_iota(jnp.int32, (ROWS, 1), 0)
                        d_low2[part] = dn[part].astype(BF16)
                        factor = factors[pair : pair + 1, 0:1]
                        d_final = jnp.where(position < lengths[pair], cot[part].astype(F32) * factor, 0.0)
                        d_after[part] = d_final
                        d_low[part] = d_final.astype(BF16)

                store = moves.start(d_low2, block_out)
                weight_grad(hidden, d_low, g_down, ff // 4, width)
                hops.ready("down")
                mlp_back(d_low, w_in, w_down, slopes, dn)
                hops.hop("down")
                store.wait()

                def finish_after(part, d_input):
                    total = d_after[part] + d_input
                    d_after[part] = total
                    d_low2[part] = total.astype(BF16)

                norm_back(dn, after, gains[2:3], gain_sum, 2, finish_after)
                d_crossed[...] = dot(d_low2[...], w_dec[:, width:], 1, 1).astype(BF16)

                @pl.loop(0, pairs)
                def _(pair):
                    part = span(pair * seq, seq)
                    attend_back(
                        queries, 0, keyval, 0, keyval, width, d_crossed,
                        (d_queries, 0), (d_keyval, 0), (d_keyval, width), seq, None, (pair, pair + 1),
                    )
                    back[part] = dot(d_keyval[part], w_enc[...], 1, 1).astype(BF16)
                    to_enc(pair).start()

                hops.hop("down")
                dn[...] = dot(d_queries[...], w_dec[:, :width], 1, 1)

                def finish_middle(part, d_input):
                    d_after[part] = d_after[part] + d_input

                norm_back(dn, middle, gains[1:2], gain_sum, 1, finish_middle)

            pl.run_scoped(
                to_memory,
                vmem(w_cross_shape, BF16), vmem(w_cross_shape, BF16), vmem(w_in_shape, BF16), vmem(w_down_shape, BF16),
                slim, broad, vmem((rows, ff), BF16), slim, broad, slim, broad,
            )

            def to_input(w_qkv, w_out, d_low, d_attended, dn, g_in, g_dec, g_enc, g_out, g_qkv):
                grads.update({"in": g_in, "crossD": g_dec, "crossE": g_enc, "out": g_out, "qkv": g_qkv})
                load_out = moves.start(out_full, w_out)
                loads = [moves.start(qkv_full, w_qkv)]
                weight_grad(normed_b, slopes, g_in, width // 3, ff // 2)
                hops.ready("in")
                joined = slopes.at[:, pl.ds(0, 3 * width)]
                loads.append(moves.start(joined_kept, joined))
                weight_grad(memory, d_keyval, g_enc, width // 3, width)
                hops.ready("crossE")
                loads.append(moves.start(x_in, memory))
                weight_grad(crossed, d_low2, g_dec, width // 3, width, column_at=width)
                load_attended = moves.start(attended_kept, crossed)
                weight_grad(normed_a, d_queries, g_dec, width // 3, width)
                hops.ready("crossD")
                load_out.wait()
                load_attended.wait()
                self_back(
                    hops, lengths, d_after, memory, normed_a, d_low, w_qkv, w_out, joined, crossed, d_attended, dn, loads,
                    ("down",), ("in", "crossE"),
                )
                store = moves.start(d_after, input_out)
                gains_ready(hops)
                hops.rest(("crossE", "down", "in", "crossD", "out", "qkv", "gains"))
                store.wait()
                for name in SCATTER_NAMES:
                    scatter.drain(name)

            pl.run_scoped(
                to_input,
                vmem(w_qkv_shape, BF16), vmem(w_out_shape, BF16), slim, slim, broad,
                *grad_space("in", "crossD", "crossE", "out", "qkv"),
            )

        pl.run_scoped(
            rest,
            slim, slim, vmem((rows, 2 * width), BF16), slim, slim, vmem((rows, 2 * ff), BF16), slim, broad,
        )
        gather.drain(names)
        for pair in range(pairs):
            to_enc(pair).wait_send()
        passed_sum.wait_send()


def run_step(wide, seq, lengths, sources, loss_weight, gains, x, cot, w_qkv, w_out, w_cross, w_in, w_down):
    (rows, width), chips, pairs = x.shape, wide // 2, x.shape[0] // seq
    vmem, shaped, dma = pltpu.VMEM, jax.ShapeDtypeStruct, pltpu.SemaphoreType.DMA
    fulls = [(wide * w.shape[0], w.shape[1]) for w in (w_qkv, w_out, w_cross, w_cross, w_in, w_down)]
    shares = [w.shape for w in (w_down, w_in, w_cross, w_cross, w_out, w_qkv)] + [BLOCK]
    types = [BF16] * 6 + [F32]
    gathered, scattered = len(GATHER_NAMES), len(SCATTER_NAMES)
    return pl.pallas_call(
        partial(step_kernel, wide, seq),
        out_shape=[shaped((wide * BLOCK[0], BLOCK[1]), F32)]
        + [shaped(f, BF16) for f in fulls]
        + [shaped((rows, 3 * width), BF16), shaped((rows, width), BF16)]
        + [shaped((rows, width), F32)] * 2
        + [shaped((rows, width), BF16), shaped((rows, width), F32)]
        + [shaped(shares[n], F32) for n in (0, 1, 2, 4, 5, 6)],
        in_specs=[SMEM] * 3 + [VMEM] + [ANY] * 7,
        out_specs=[ANY] * 13 + [VMEM] * 6,
        scratch_shapes=[
            vmem(BLOCK, F32),
            vmem((BLOCK[0], width), F32),
            vmem(BLOCK, F32),
            vmem((3, 8, width), F32),
            vmem((rows, width), BF16),
            vmem((rows, width), BF16),
            vmem(w_cross.shape, F32),
            vmem(w_cross.shape, F32),
            vmem((wide * BLOCK[0], BLOCK[1]), F32),
            vmem(fulls[5], BF16),
        ]
        + [vmem((chips,) + s, t) for s, t in zip(shares, types)]
        + [vmem((chips - 1,) + s, t) for s, t in zip(shares, types)]
        + [dma((64,)), dma((2 + 2 * pairs,)), dma((2 + 2 * pairs,))]
        + [dma((gathered,)), dma((gathered, 2, chips // 2)), dma((gathered, 2, chips // 2))]
        + [dma((gathered, chips)), dma((gathered, chips)), dma((scattered, chips)), dma((scattered, chips))]
        + [dma((scattered, 2, chips // 2)), dma((scattered, 2, chips // 2))],
        name="encoder_and_decoder",
        compiler_params=pltpu.CompilerParams(collective_id=0, has_side_effects=True, vmem_limit_bytes=VMEM_LIMIT),
    )(lengths, sources, loss_weight, gains, x, cot, w_qkv, w_out, w_cross, w_in, w_down)


def copy_kernel(count, *refs):
    blocks, gains, stored, gains_out = refs[:count], refs[count], refs[count + 1 : 2 * count + 1], refs[2 * count + 1]
    held, sems = refs[2 * count + 2 : -1], refs[-1]
    loads = [pltpu.make_async_copy(blocks[n], held[n], sems.at[n]) for n in range(count)]
    stores = [pltpu.make_async_copy(held[n], stored[n], sems.at[count + n]) for n in range(count)]
    for load in loads:
        load.start()
    gains_out[...] = gains[0 : gains_out.shape[0], 0 : gains_out.shape[1]]
    for load, store in zip(loads, stores):
        load.wait()
        store.start()
    for store in stores:
        store.wait()


def copied(arrays, gains, gains_shape):
    count = len(arrays)
    return pl.pallas_call(
        partial(copy_kernel, count),
        out_shape=[jax.ShapeDtypeStruct(a.shape, a.dtype) for a in arrays] + [jax.ShapeDtypeStruct(gains_shape, F32)],
        in_specs=[ANY] * count + [VMEM],
        out_specs=[ANY] * count + [VMEM],
        scratch_shapes=[pltpu.VMEM(a.shape, a.dtype) for a in arrays] + [pltpu.SemaphoreType.DMA((2 * count,))],
        name="outputs",
    )(*arrays, gains)


def shifted(block, axis, distance):
    devices = range(lax.axis_size(axis))
    route = [(i - distance, i) for i in devices if i - distance in devices]
    return lax.ppermute(block, axis, route)


def plain_product(a, b):
    return jnp.dot(a, b, preferred_element_type=jnp.float32)


def plain_split_heads(v):
    return v.reshape(v.shape[0], HEADS, -1)


def plain_norm_forward(h, norm_gain):
    inv_root = lax.rsqrt(jnp.mean(h * h, axis=-1, keepdims=True) + EPS)
    return (h * inv_root * norm_gain.astype(jnp.float32), inv_root)


def plain_norm_back(d_normed, h, inv_root, norm_gain):
    scaled = h * inv_root
    d_gain = jnp.sum(d_normed * scaled, axis=0)
    inner = d_normed * norm_gain.astype(jnp.float32)
    d_input = inv_root * (inner - scaled * jnp.mean(inner * scaled, axis=-1, keepdims=True))
    return (d_input, d_gain)


def plain_score_block(q, k, key_mask):
    scores = jnp.einsum(
        "qhd,khd->hqk", plain_split_heads(q), plain_split_heads(k), preferred_element_type=jnp.float32
    ) * HEAD_DIM ** (-0.5)
    if key_mask is not None:
        scores = jnp.where(key_mask[None], scores, NEG)
    return scores


def plain_attend_forward(q, k, v, key_mask):
    scores = plain_score_block(q, k, key_mask)
    highest = jnp.max(scores, axis=-1, keepdims=True)
    expo = jnp.exp(scores - highest)
    total = jnp.sum(expo, axis=-1, keepdims=True)
    weights = (expo / total).astype(jnp.bfloat16)
    output = jnp.einsum("hqk,khd->qhd", weights, plain_split_heads(v), preferred_element_type=jnp.float32)
    return (output.reshape(q.shape[0], -1), highest + jnp.log(total))


def plain_attend_back(q, k, v, key_mask, log_total, d_out):
    scores = plain_score_block(q, k, key_mask)
    probs = jnp.exp(scores - log_total)
    heads_dout = plain_split_heads(d_out)
    d_value = jnp.einsum(
        "hqk,qhd->khd", probs.astype(jnp.bfloat16), heads_dout, preferred_element_type=jnp.float32
    )
    d_probs = jnp.einsum(
        "qhd,khd->hqk", heads_dout, plain_split_heads(v), preferred_element_type=jnp.float32
    )
    centre = jnp.sum(probs * d_probs, axis=-1, keepdims=True)
    d_scores = (probs * (d_probs - centre)).astype(jnp.bfloat16)
    d_query = jnp.einsum(
        "hqk,khd->qhd", d_scores, plain_split_heads(k), preferred_element_type=jnp.float32
    ) * HEAD_DIM ** (-0.5)
    d_key = jnp.einsum(
        "hqk,qhd->khd", d_scores, plain_split_heads(q), preferred_element_type=jnp.float32
    ) * HEAD_DIM ** (-0.5)
    rows_query = q.shape[0]
    rows_key = k.shape[0]
    return (
        d_query.reshape(rows_query, -1),
        d_key.reshape(rows_key, -1),
        d_value.reshape(rows_key, -1),
    )


def plain_attention_forward(h, norm_gain, w_qkv, w_out, key_mask):
    normed, inv_root = plain_norm_forward(h, norm_gain)
    normed_low = normed.astype(jnp.bfloat16)
    joined = plain_product(normed_low, w_qkv).astype(jnp.bfloat16)
    q, k, v = jnp.split(joined, 3, axis=1)
    output, log_total = plain_attend_forward(q, k, v, key_mask)
    output_low = output.astype(jnp.bfloat16)
    return (normed_low, inv_root, joined, output_low, log_total, plain_product(output_low, w_out))


def plain_attention_back(d_h, h, saved, norm_gain, w_qkv, w_out, key_mask):
    normed_low, inv_root, joined, output_low, log_total, unused = saved
    d_low = d_h.astype(jnp.bfloat16)
    d_wout = plain_product(output_low.T, d_low)
    d_output = plain_product(d_low, w_out.T).astype(jnp.bfloat16)
    q, k, v = jnp.split(joined, 3, axis=1)
    d_query, d_key, d_value = plain_attend_back(q, k, v, key_mask, log_total, d_output)
    d_joined = jnp.concatenate([d_query, d_key, d_value], axis=1).astype(jnp.bfloat16)
    d_wqkv = plain_product(normed_low.T, d_joined)
    d_normed = plain_product(d_joined, w_qkv.T)
    d_input, d_gain = plain_norm_back(d_normed, h, inv_root, norm_gain)
    return (d_input, d_gain, d_wqkv, d_wout)


def plain_mlp_forward(h, norm_gain, w_in, w_down):
    normed, inv_root = plain_norm_forward(h, norm_gain)
    normed_low = normed.astype(jnp.bfloat16)
    joined = plain_product(normed_low, w_in)
    gate, upper = jnp.split(joined, 2, axis=1)
    hidden_low = (jax.nn.gelu(gate, approximate=True) * upper).astype(jnp.bfloat16)
    return (normed_low, inv_root, joined, hidden_low, plain_product(hidden_low, w_down))


def plain_mlp_back(d_h, h, saved, norm_gain, w_in, w_down):
    normed_low, inv_root, joined, hidden_low, unused = saved
    d_low = d_h.astype(jnp.bfloat16)
    d_wdown = plain_product(hidden_low.T, d_low)
    d_hidden = plain_product(d_low, w_down.T)
    gate, upper = jnp.split(joined, 2, axis=1)
    active, active_back = jax.vjp(partial(jax.nn.gelu, approximate=True), gate)
    d_gate = active_back(d_hidden * upper)[0]
    d_upper = d_hidden * active
    d_joined = jnp.concatenate([d_gate, d_upper], axis=1).astype(jnp.bfloat16)
    d_win = plain_product(normed_low.T, d_joined)
    d_normed = plain_product(d_joined, w_in.T)
    d_input, d_gain = plain_norm_back(d_normed, h, inv_root, norm_gain)
    return (d_input, d_gain, d_win, d_wdown)


def encoder_forward(weights, source):
    gains, w_qkv, w_out, w_cross, w_in, w_down = weights
    inputs = source.astype(jnp.float32)
    attn_saved = plain_attention_forward(inputs, gains[0], w_qkv, w_out, None)
    middle = inputs + attn_saved[-1]
    mlp_saved = plain_mlp_forward(middle, gains[1], w_in, w_down)
    final = middle + mlp_saved[-1]
    normed, inv_root = plain_norm_forward(final, gains[2])
    memory = normed.astype(jnp.bfloat16)
    key_value = plain_product(memory, w_cross).astype(jnp.bfloat16)
    return (inputs, attn_saved, middle, mlp_saved, final, inv_root, memory, key_value)


def encoder_front(weights, source):
    saved = encoder_forward(weights, source)
    return (saved[7], saved[6])


def encoder_back_saved(weights, saved, d_keyvalue):
    gains, w_qkv, w_out, w_cross, w_in, w_down = weights
    inputs, attn_saved, middle, mlp_saved, final, inv_root, memory, key_value = saved
    d_wcross = plain_product(memory.T, d_keyvalue)
    d_memory = plain_product(d_keyvalue, w_cross.T)
    d_final, gain_last = plain_norm_back(d_memory, final, inv_root, gains[2])
    d_part, gain_mlp, d_win, d_wdown = plain_mlp_back(d_final, middle, mlp_saved, gains[1], w_in, w_down)
    d_middle = d_final + d_part
    d_first, gain_attn, d_wqkv, d_wout = plain_attention_back(
        d_middle, inputs, attn_saved, gains[0], w_qkv, w_out, None
    )
    grads = (jnp.stack([gain_attn, gain_mlp, gain_last]), d_wqkv, d_wout, d_wcross, d_win, d_wdown)
    return (d_middle + d_first, grads)


def encoder_back(weights, source, d_keyvalue):
    return encoder_back_saved(weights, encoder_forward(weights, source), d_keyvalue)


def decoder_pass(weights, source, key_value, weight_cot, length, factor):
    gains, w_qkv, w_out, w_cross, w_in, w_down = weights
    width = source.shape[1]
    inputs = source.astype(jnp.float32)
    position = jnp.arange(inputs.shape[0], dtype=jnp.int32)
    is_valid = position < length
    key_mask = (position[None, :] <= position[:, None]) & is_valid[None, :]
    attn_saved = plain_attention_forward(inputs, gains[0], w_qkv, w_out, key_mask)
    middle = inputs + attn_saved[-1]
    normed, inv_root = plain_norm_forward(middle, gains[1])
    normed_low = normed.astype(jnp.bfloat16)
    w_query = w_cross[:, :width]
    w_back = w_cross[:, width:]
    queries = plain_product(normed_low, w_query).astype(jnp.bfloat16)
    mem_keys = key_value[:, :width]
    mem_values = key_value[:, width:]
    cross_out, cross_total = plain_attend_forward(queries, mem_keys, mem_values, None)
    cross_low = cross_out.astype(jnp.bfloat16)
    after = middle + plain_product(cross_low, w_back)
    mlp_saved = plain_mlp_forward(after, gains[2], w_in, w_down)
    final = after + mlp_saved[-1]
    d_final = jnp.where(is_valid[:, None], weight_cot.astype(jnp.float32) * factor, 0.0)
    d_part, gain_mlp, d_win, d_wdown = plain_mlp_back(d_final, after, mlp_saved, gains[2], w_in, w_down)
    d_after = d_final + d_part
    d_low = d_after.astype(jnp.bfloat16)
    d_wback = plain_product(cross_low.T, d_low)
    d_cross = plain_product(d_low, w_back.T).astype(jnp.bfloat16)
    d_query, d_key, d_value = plain_attend_back(queries, mem_keys, mem_values, None, cross_total, d_cross)
    d_query_low = d_query.astype(jnp.bfloat16)
    d_wquery = plain_product(normed_low.T, d_query_low)
    d_normed = plain_product(d_query_low, w_query.T)
    d_norm_in, gain_cross = plain_norm_back(d_normed, middle, inv_root, gains[1])
    d_middle = d_after + d_norm_in
    d_keyvalue = jnp.concatenate([d_key, d_value], axis=1).astype(jnp.bfloat16)
    d_first, gain_attn, d_wqkv, d_wout = plain_attention_back(
        d_middle, inputs, attn_saved, gains[0], w_qkv, w_out, key_mask
    )
    grads = (
        jnp.stack([gain_attn, gain_cross, gain_mlp]),
        d_wqkv,
        d_wout,
        jnp.concatenate([d_wquery, d_wback], axis=1),
        d_win,
        d_wdown,
    )
    return (final.astype(jnp.bfloat16), d_middle + d_first, d_keyvalue, grads)


def on_section(flag, work, operands):

    def run_work(values):
        return work(*values)

    def skip_work(values):
        return jax.tree.map(jnp.zeros_like, work(*values))

    return lax.cond(flag, run_work, skip_work, operands)


def plain_body(
    block_in,
    cotangent,
    lengths,
    sources,
    loss_weight,
    gains,
    qkv_weight,
    out_weight,
    cross_weight,
    in_weight,
    down_weight,
):
    is_encoder = lax.axis_index("section") == 0
    is_decoder = jnp.logical_not(is_encoder)
    wide = lax.axis_size("dp")
    gathered = (
        lax.all_gather(gains, "dp", axis=2, tiled=True),
        lax.all_gather(qkv_weight, "dp", axis=1, tiled=True),
        lax.all_gather(out_weight, "dp", axis=1, tiled=True),
        lax.all_gather(cross_weight, "dp", axis=1, tiled=True),
        lax.all_gather(in_weight, "dp", axis=1, tiled=True),
        lax.all_gather(down_weight, "dp", axis=1, tiled=True),
    )
    weights = tuple((w[0] for w in gathered))
    onehot = (sources[:, None] == jnp.arange(3, dtype=jnp.int32)[None, :]).astype(jnp.float32)
    counts = lax.psum(jnp.sum(onehot * lengths[:, None].astype(jnp.float32), axis=0), "dp")
    own_count = jnp.sum(onehot * counts[None, :], axis=1)
    own_weight = jnp.sum(onehot * loss_weight[None, :].astype(jnp.float32), axis=1)
    scale = own_weight * (lengths.shape[0] * wide * block_in.shape[2] / 3.0) / own_count

    def step(carry, item):
        source, weight_cot, length, factor = item
        key_value, memory = on_section(is_encoder, encoder_front, (weights, source))
        received = shifted(key_value, "section", 1)
        decoded, table_grad, d_keyvalue, dec_grads = on_section(
            is_decoder, decoder_pass, (weights, source, received, weight_cot, length, factor)
        )
        returned = shifted(d_keyvalue, "section", -1)
        plot_grad, enc_grads = on_section(is_encoder, encoder_back, (weights, source, returned))
        grads = tuple((a + b for a, b in zip(dec_grads, enc_grads)))
        carry = tuple((a + b for a, b in zip(carry, grads)))
        return (carry, (memory + decoded, plot_grad + table_grad))

    start = tuple((jnp.zeros(w.shape, jnp.float32) for w in weights))
    carry, (outputs, input_grads) = lax.scan(step, start, (block_in[0], cotangent, lengths, scale))
    gain_total, qkv_total, out_total, cross_sum, in_total, down_total = carry
    reduced = (
        lax.psum_scatter(gain_total[None], "dp", scatter_dimension=2, tiled=True),
        lax.psum_scatter(qkv_total[None], "dp", scatter_dimension=1, tiled=True),
        lax.psum_scatter(out_total[None], "dp", scatter_dimension=1, tiled=True),
        lax.psum_scatter(cross_sum[None], "dp", scatter_dimension=1, tiled=True),
        lax.psum_scatter(in_total[None], "dp", scatter_dimension=1, tiled=True),
        lax.psum_scatter(down_total[None], "dp", scatter_dimension=1, tiled=True),
    )
    return (
        outputs[None],
        input_grads[None],
        reduced[0],
        reduced[1],
        reduced[2],
        reduced[3],
        reduced[4],
        reduced[5],
    )


def tiled_body(
    block_in, cotangent, lengths, sources, loss_weight, gains, qkv_weight, out_weight, cross_weight, in_weight, down_weight
):
    wide = lax.axis_size("dp")
    pairs, seq, width = block_in.shape[1:]
    x, cot = block_in.reshape(pairs * seq, width), cotangent.reshape(pairs * seq, width)
    results = run_step(
        wide, seq, lengths, sources, loss_weight, gains[0], x, cot,
        qkv_weight[0], out_weight[0], cross_weight[0], in_weight[0], down_weight[0],
    )
    block_out, input_grad, down, inner, cross, out, qkv, gains_sum = copied(results[-8:-1], results[-1], gains.shape[1:])
    return (
        block_out.reshape(block_in.shape),
        input_grad.reshape(block_in.shape),
        gains_sum[None],
        qkv[None],
        out[None],
        cross[None],
        inner[None],
        down[None],
    )


def solution(mesh):
    in_specs = (
        P("section", "dp", None, None),
        P("dp", None, None),
        P("dp"),
        P("dp"),
        P(),
        P("section", None, "dp"),
        P("section", "dp", None),
        P("section", "dp", None),
        P("section", "dp", None),
        P("section", "dp", None),
        P("section", "dp", None),
    )
    out_specs = (
        P("section", "dp", None, None),
        P("section", "dp", None, None),
        P("section", None, "dp"),
        P("section", "dp", None),
        P("section", "dp", None),
        P("section", "dp", None),
        P("section", "dp", None),
        P("section", "dp", None),
    )

    def body(*args):
        shards = args[6:]
        tiled = args[5].shape[2] <= 128 and all(w.shape[1] % 16 == 0 for w in shards)
        return (tiled_body if tiled else plain_body)(*args)

    return jax.shard_map(body, mesh=mesh, in_specs=in_specs, out_specs=out_specs, check_vma=False)
```

profile of v0, /device:TPU:0, one launch (start us, length us, event | category | flops | bytes accessed | tf_op | source)
XLA Modules:
  0.0 255.0 jit_solution(14484880212860260984)
XLA Ops:
  0.6 248.2 %encoder_and_decoder.1 = (f32[128,128]{1,0:T(8,128)}, bf16[768,2304]{1,0:T(8,128)(2,1)}, bf16[768,768]{1,0:T(8,128)(2,1)}, bf16[768,1536]{1,0:T(8,128)(2,1)}, bf...) custom-call(s32[2]{0:T(128)} %lengths.1, ...), custom_call_target="tpu_custom_call" | custom-call | tf_op jit(solution)/shard_map/encoder_and_decoder/pallas_call | solution.py:879
  248.9 4.8 %outputs.1 = (bf16[512,768]{1,0:T(8,128)(2,1)}, f32[512,768]{1,0:T(8,128)}, f32[128,768]{1,0:T(8,128)}, f32[48,4096]{1,0:T(8,128)}, f32[48,1536]{1,0:T(8,128)}, ...) custom-call(bf16[512,768]{1,0:T(8,128)(2,1)} %get-tuple-element.24.refs_0_, ...), custom_call_target="tpu_custom_call" | custom-call | tf_op jit(solution)/shard_map/outputs/pallas_call | solution.py:929
  253.7 1.2 copy.19
where the time goes:
time: 255 us
  Pallas kernels  253 us (99%)
    pallas_call x1, Pallas kernels, run_step(): pl.pallas_call(partial(step_kernel, wide, seq), out_shape=[shaped((wide *...  248 us

commit v1 on v0

--- a/solution.py
+++ b/solution.py
@@ -910,16 +910,20 @@
 
 
 def copy_kernel(count, *refs):
-    blocks, gains, stored, gains_out = refs[:count], refs[count], refs[count + 1 : 2 * count + 1], refs[2 * count + 1]
-    held, sems = refs[2 * count + 2 : -1], refs[-1]
-    loads = [pltpu.make_async_copy(blocks[n], held[n], sems.at[n]) for n in range(count)]
-    stores = [pltpu.make_async_copy(held[n], stored[n], sems.at[count + n]) for n in range(count)]
-    for load in loads:
-        load.start()
-    gains_out[...] = gains[0 : gains_out.shape[0], 0 : gains_out.shape[1]]
-    for load, store in zip(loads, stores):
-        load.wait()
-        store.start()
+    sources, goals = refs[: count + 1], refs[count + 1 : 2 * count + 2]
+    held, gains_own, sems = refs[2 * count + 2 : -2], refs[-2], refs[-1]
+    loads = [pltpu.make_async_copy(a, b, sems.at[n]) for n, (a, b) in enumerate(zip(sources, held))]
+    stores = [
+        pltpu.make_async_copy(a, b, sems.at[count + 1 + n]) for n, (a, b) in enumerate(zip((*held[:count], gains_own), goals))
+    ]
+    order = [count, *range(count)]
+    for n in order:
+        loads[n].start()
+    for n in order:
+        loads[n].wait()
+        if n == count:
+            gains_own[0] = held[count][0 : gains_own.shape[1], 0 : gains_own.shape[2]]
+        stores[n].start()
     for store in stores:
         store.wait()
 
@@ -929,9 +933,10 @@
     return pl.pallas_call(
         partial(copy_kernel, count),
         out_shape=[jax.ShapeDtypeStruct(a.shape, a.dtype) for a in arrays] + [jax.ShapeDtypeStruct(gains_shape, F32)],
-        in_specs=[ANY] * count + [VMEM],
-        out_specs=[ANY] * count + [VMEM],
-        scratch_shapes=[pltpu.VMEM(a.shape, a.dtype) for a in arrays] + [pltpu.SemaphoreType.DMA((2 * count,))],
+        in_specs=[ANY] * (count + 1),
+        out_specs=[ANY] * (count + 1),
+        scratch_shapes=[pltpu.VMEM(a.shape, a.dtype) for a in (*arrays, gains)]
+        + [pltpu.VMEM(gains_shape, F32), pltpu.SemaphoreType.DMA((2 * count + 2,))],
         name="outputs",
     )(*arrays, gains)
 
@@ -1231,11 +1236,11 @@
         wide, seq, lengths, sources, loss_weight, gains[0], x, cot,
         qkv_weight[0], out_weight[0], cross_weight[0], in_weight[0], down_weight[0],
     )
-    block_out, input_grad, down, inner, cross, out, qkv, gains_sum = copied(results[-8:-1], results[-1], gains.shape[1:])
+    block_out, input_grad, down, inner, cross, out, qkv, gains_sum = copied(results[-8:-1], results[-1], gains.shape)
     return (
         block_out.reshape(block_in.shape),
         input_grad.reshape(block_in.shape),
-        gains_sum[None],
+        gains_sum,
         qkv[None],
         out[None],
         cross[None],

time: 255 us -> 254 us (level)
  no operation moved by 1% of the time
where the time goes in v1:
time: 254 us
  Pallas kernels  252 us (99%)
    pallas_call x1, Pallas kernels, run_step(): pl.pallas_call(partial(step_kernel, wide, seq), out_shape=[shaped((wide *...  248 us

profile of v1, /device:TPU:0, one launch (start us, length us, event | category | flops | bytes accessed | tf_op | source)
XLA Modules:
  0.0 253.7 jit_solution(5680827936672917183)
XLA Ops:
  0.6 248.2 %encoder_and_decoder.1 = (f32[128,128]{1,0:T(8,128)}, bf16[768,2304]{1,0:T(8,128)(2,1)}, bf16[768,768]{1,0:T(8,128)(2,1)}, bf16[768,1536]{1,0:T(8,128)(2,1)}, bf...) custom-call(s32[2]{0:T(128)} %lengths.1, ...), custom_call_target="tpu_custom_call" | custom-call | tf_op jit(solution)/shard_map/encoder_and_decoder/pallas_call | solution.py:879
  248.9 3.6 %outputs.1 = (bf16[512,768]{1,0:T(8,128)(2,1)}, f32[512,768]{1,0:T(8,128)}, f32[128,768]{1,0:T(8,128)}, f32[48,4096]{1,0:T(8,128)}, f32[48,1536]{1,0:T(8,128)}, ...) custom-call(bf16[512,768]{1,0:T(8,128)(2,1)} %get-tuple-element.24.refs_0_, ...), custom_call_target="tpu_custom_call" | custom-call | tf_op jit(solution)/shard_map/outputs/pallas_call | solution.py:933
  252.5 1.2 copy.19
